TPU v7x, 32 devices: a whole 2x2x4 slice. The times are simulated.
32 devices in a mesh: group: 4 (over x, core), tp: 8 (over z, y).
Axes of the slice: x: 2, y: 2, z: 4, core: 2. Of those that a mesh axis runs over, the one named last changes fastest.
Arguments:
- hidden: bfloat16 [4096, 28672], P('group', 'tp'), may hold values from -6 to 6
- residual: bfloat16 [4096, 8192], P('group', 'tp'), may hold values from -6 to 6
- down_projection_weight: bfloat16 [28672, 8192], P('tp'), may hold values from -0.03125 to 0.03125
- adapter_down_maps: bfloat16 [128, 64, 28672], P('group', None, 'tp'), may hold values from -0.03125 to 0.03125
- adapter_up_maps: bfloat16 [128, 64, 8192], P('group', None, 'tp'), may hold values from -0.75 to 0.75
- row_adapter_index: int32 [4096, 1], P('group'), may hold values from 0 to 127; in each aligned block of 1024 rows (0 to 1023, 1024 to 2047, ...) at most 16 rows name the same one
Outputs:
- layer_out: bfloat16 [4096, 8192], P('group', 'tp')
Inputs may be any that keep to these rules, and one draw needn't show every extreme that they name: `row_adapter_index`: within the 1024 rows of one group no adapter is named by more than 16 rows; in some group some adapter is named by exactly 16 rows; every adapter is named by some row.
All inputs are finite; a program needn't handle non-finite values.
Results may differ from a plain program's by a relative error of at most 0.02.
Values may be sent and summed in bfloat16 or wider, within the bound.
A program may use at most 256 MiB of HBM per device.

v0:
```python
import jax
import jax.numpy as jnp
from jax import lax
from jax.sharding import PartitionSpec as P

MOST = 16


def per_device(
    hidden, residual, down_projection_weight, adapter_down_maps, adapter_up_maps, row_adapter_index
):
    group_count = lax.axis_size("group")
    hidden_cols = hidden.shape[1]
    feature_cols = residual.shape[1]
    resident_adapters = adapter_down_maps.shape[0]
    adapter_total = resident_adapters * group_count
    rank_columns = adapter_down_maps.shape[1]
    row_adapter = row_adapter_index[:, 0]
    one_hot = (row_adapter[:, None] == jnp.arange(adapter_total, dtype=jnp.int32)[None, :]).astype(
        jnp.int32
    )
    before = jnp.cumsum(one_hot, axis=0) - 1
    slot_rank = jnp.sum(one_hot * before, axis=1)
    slot_index = row_adapter * MOST + slot_rank
    parcels_flat = (
        jnp.zeros((adapter_total * MOST, hidden_cols), jnp.bfloat16).at[slot_index].set(hidden)
    )
    base_cols = lax.psum_scatter(
        lax.dot_general(
            down_projection_weight,
            hidden,
            (((0,), (1,)), ((), ())),
            preferred_element_type=jnp.float32,
        ).astype(jnp.bfloat16),
        "tp",
        scatter_dimension=0,
        tiled=True,
    ).astype(jnp.float32)
    every_a, every_b = (
        lax.all_gather(adapter_down_maps, "group", axis=0, tiled=True),
        lax.all_gather(adapter_up_maps, "group", axis=0, tiled=True),
    )
    local_slots = parcels_flat.reshape(adapter_total, MOST, hidden_cols)
    partial_mix = jnp.einsum(
        "amf,arf->amr", local_slots, every_a, preferred_element_type=jnp.float32
    )
    summed = lax.psum(partial_mix.reshape(adapter_total, MOST * rank_columns), "tp")
    rank_mix = summed.reshape(adapter_total, MOST, rank_columns).astype(jnp.bfloat16)
    delta_slots = jnp.einsum("amr,ard->amd", rank_mix, every_b, preferred_element_type=jnp.float32)
    delta_slots = delta_slots.astype(jnp.bfloat16).reshape(adapter_total * MOST, feature_cols)
    delta_rows = delta_slots[slot_index]
    total = residual.astype(jnp.float32) + base_cols.T + delta_rows.astype(jnp.float32)
    return total.astype(jnp.bfloat16)


def solution(mesh):
    in_specs = (
        P("group", "tp"),
        P("group", "tp"),
        P("tp", None),
        P("group", None, "tp"),
        P("group", None, "tp"),
        P("group", None),
    )
    out_specs = P("group", "tp")
    return jax.shard_map(
        per_device, mesh=mesh, in_specs=in_specs, out_specs=out_specs, check_vma=False
    )
```

profile of v0, /device:TPU:0, one launch (start us, length us, event | category | flops | bytes accessed | tf_op | source)
XLA Modules:
  0.0 500.8 jit_solution(4180529954436930982)
XLA Ops:
  7.4 0.0 all-gather.3.cloned.1.call-start
  7.4 0.7 all-gather.3.cloned.1.call-update
  8.1 0.0 all-gather.5.cloned.1.call-start
  8.1 0.7 all-gather.5.cloned.1.call-update
  8.8 0.0 reduce-scatter.2.cloned.1.call-start
  8.9 68.9 %convolution_convert_fusion = bf16[8192,1024]{1,0:T(8,128)(2,1)} fusion(bf16[3584,8192]{1,0:T(8,128)(2,1)} %param.8, bf16[1024,3584]{1,0:T(8,128)(2,1)} %param.6), kind=kOutput, calls=%fused_computation.2 | convolution fusion | flops 60137930752 | bytes 82837504 | tf_op jit(solution)/shard_map/dot_general | solution.py:29
  77.8 0.0 copy-start.1
  77.8 0.0 copy-start
  77.8 0.0 reduce-scatter.2.cloned.1.call-update
  77.8 0.7 copy-done.1
  78.4 0.1 copy.19
  78.5 0.2 fusion.5
  78.8 0.1 copy.20
  78.9 0.4 copy-done
  79.4 2.6 copy.18
  81.9 0.4 fusion.4
  82.3 19.7 %scatter_custom_fusion = bf16[2048,3584]{1,0:T(8,128)(2,1)} fusion(s32[1024]{0:T(1024)S(1)} %bitcast.35, bf16[1024,3584]{1,0:T(8,128)(2,1)} %param.6, bf16[]{:T(256)} %constant.5.clone.1), kind=kCustom, calls=%fused_computation.3 | custom fusion | bytes 14680576 | tf_op jit(solution)/shard_map/scatter | solution.py:26
  102.0 256.6 %all-gather.3.cloned.1.call-done = bf16[128,64,3584]{2,1,0:T(8,128)(2,1)} async-done(((bf16[32,64,3584]{2,1,0:T(8,128)(2,1)}), bf16[128,64,3584]{2,1,0:T(8,128)(2,1)}) %all-gather.3.cloned.1.call-update) | async-done | bytes 58720272 | tf_op jit(solution)/shard_map/all_gather | solution.py:40
  358.6 31.0 %fusion.8 = f32[128,16,64]{2,1,0:T(8,128)S(1)} fusion(bf16[128,16,3584]{2,1,0:T(8,128)(2,1)} %bitcast.29, bf16[128,64,3584]{2,1,0:T(8,128)(2,1)} %all-gather.3.cloned.1.call-done), kind=kOutput, calls=%fused_computation.20 | convolution fusion | flops 939524096 | bytes 73924608 | tf_op jit(solution)/shard_map/amf,arf->amr/dot_general | solution.py:44
  389.6 0.4 copy.21
  390.0 43.1 %all-reduce.1 = bf16[128,1024]{0,1:T(8,128)(2,1)S(1)} all-reduce(f32[128,1024]{0,1:T(8,128)S(1)} %bitcast.30), channel_id=1, replica_groups=mesh['group'=4,'tp'=8] {'tp'}, use_global_device_ids=true, to_apply=%region_5.6 | all-reduce | flops 131072 | bytes 786432 | tf_op jit(solution)/shard_map/psum | solution.py:47
  433.1 0.4 copy.22
  433.6 32.6 %all-gather.5.cloned.1.call-done = bf16[128,64,1024]{2,1,0:T(8,128)(2,1)} async-done(((bf16[32,64,1024]{2,1,0:T(8,128)(2,1)}), bf16[128,64,1024]{2,1,0:T(8,128)(2,1)}) %all-gather.5.cloned.1.call-update) | async-done | bytes 16777232 | tf_op jit(solution)/shard_map/all_gather | solution.py:41
  466.2 10.0 %convolution_convert_fusion.1 = bf16[128,16,1024]{2,1,0:T(8,128)(2,1)} fusion(bf16[128,16,64]{2,1,0:T(8,128)(2,1)S(1)} %copy.22, bf16[128,64,1024]{2,1,0:T(8,128)(2,1)} %all-gather.5.cloned.1.call-done), kind=kOutput, calls=%fused_computation.8 | convolution fusion | flops 270532608 | bytes 21233664 | tf_op jit(solution)/shard_map/amr,ard->amd/dot_general | solution.py:49
  476.2 7.7 %gather_fusion = bf16[1024,1024]{1,0:T(8,128)(2,1)S(1)} fusion(bf16[2048,1024]{1,0:T(8,128)(2,1)} %bitcast.28, s32[1024]{0:T(1024)S(1)} %broadcast_clamp_fusion), kind=kCustom, calls=%fused_computation | custom fusion | bytes 4198400 | tf_op jit(solution)/shard_map/gather | solution.py:51
  483.9 2.6 copy.23
  486.5 0.0 reduce-scatter.2.cloned.1.call-done
  486.5 4.3 fusion.3
  490.8 2.6 copy.24
  (6 shorter events, 0.1 us)
Async XLA Ops:
  7.4 351.2 %all-gather.3.cloned.1.call-start = ((), (), s32[]{:S(2)}) async-start(), calls=%async_computation.2 | async-start | bytes 73400320 | tf_op jit(solution)/shard_map/all_gather | solution.py:40
  8.1 458.1 %all-gather.5.cloned.1.call-start = ((), (), s32[]{:S(2)}) async-start(), calls=%async_computation.3 | async-start | bytes 20971520 | tf_op jit(solution)/shard_map/all_gather | solution.py:41
  8.8 477.6 %reduce-scatter.2.cloned.1.call-start = ((), (), s32[]{:S(2)}) async-start(), calls=%async_computation.1 | async-start | bytes 18874368 | tf_op jit(solution)/shard_map/reduce_scatter | solution.py:28
  77.8 0.7 copy-start.1
  77.8 1.6 copy-start
Sparse Core Ops, SparseCore 0:
  9.8 348.6 all-gather.2
  360.2 105.9 all-gather.4
Sparse Core Ops, SparseCore 1:
  77.9 282.4 reduce-scatter.1
where the time goes:
time: 501 us
  waiting for transfers between devices  291 us (58%)
  matrix products  110 us (22%)
  blocking collectives  43.1 us (9%)
  local copies, waits for them, and re-layouts  37.2 us (7%)
  between operations  14.9 us (3%)
    all_gather x1, waiting for transfers between devices, per_device(): lax.all_gather(adapter_down_maps, 'group', axis=0, tiled=True)  257 us
    dot_general x1, matrix products, per_device(): lax.dot_general(down_projection_weight, hidden, (((0,), (1,)), ((), ())),...  68.9 us
    psum x1, blocking collectives, per_device(): lax.psum(partial_mix.reshape(adapter_total, MOST * rank_columns), 'tp')  43.1 us
    all_gather x1, waiting for transfers between devices, per_device(): lax.all_gather(adapter_up_maps, 'group', axis=0, tiled=True)  32.6 us
    dot_general x1, matrix products, per_device(): jnp.einsum('amf,arf->amr', local_slots, every_a, preferred_element_type=j...  31 us
    scatter x1, local copies, waits for them, and re-layouts, per_device(): jnp.zeros((adapter_total * MOST, hidden_cols), jnp.bfloat16).at[slot_index]  19.7 us
    gather x2, local copies, waits for them, and re-layouts, per_device(): delta_rows = delta_slots[slot_index]  10.3 us
  transfers between devices with their start and end apart: 3, of which 2 were waited for; matrix products, arithmetic and copies ran while one was open for 29% of the time, Pallas kernels for 0%

commit v1 on v0

v1 whole, which is shorter than its diff:
```python
import functools

import jax
import jax.numpy as jnp
from jax import lax
from jax.experimental import pallas as pl
from jax.experimental.pallas import tpu as pltpu
from jax.sharding import PartitionSpec as P

MESH = pl.DeviceIdType.MESH
F32 = jnp.float32
BF16 = jnp.bfloat16
X_PARTS = 4


def kernel(
    n, groups, rank, tile,
    idr, idc, hid, res, w, a, b,
    out, xh, asib, bsib,
    hv, wv, pv, ring, av, xv, acc, ev, rv, dsend, drecv, mixb, rs, ag,
    ring_send, ring_recv, w_sem, a_sem, x_send, x_recv, sib_send, sib_recv,
    rs_send, rs_recv, ag_send, ag_recv, d_send, d_recv, loc, out_sem,
):
    rows, depth = hid.shape
    feats = res.shape[1]
    half = feats // 2
    a_rows = a.shape[0]
    tiles = a_rows // tile
    per_tile = tile // rank
    residents = a_rows // rank
    part = rows // X_PARTS
    sub = rows // 2
    block = 2 * rows // n
    blocks = n // 2

    t, g = lax.axis_index("tp"), lax.axis_index("group")
    z, y = t // 2, lax.rem(t, 2)
    pos = z + y * (n - 1 - 2 * z)

    def at(p):
        p = lax.rem(p + 2 * n, n)
        c = p // (n // 2)
        return 2 * p * (1 - c) + c * (2 * (n - 1 - p) + 1)

    toward = (at(pos + 1), at(pos - 1))
    across = lax.rem(g + groups // 2, groups)
    sibling = g + 1 - 2 * lax.rem(g, 2)

    barrier = pltpu.get_barrier_semaphore()
    for k in range(1, n):
        pl.semaphore_signal(
            barrier, inc=1, device_id=(g, lax.rem(t + k, n)), device_id_type=MESH
        )
    for other in (across, sibling):
        pl.semaphore_signal(barrier, inc=1, device_id=(other, t), device_id_type=MESH)

    own_copy = pltpu.make_async_copy(hid, hv, loc.at[0])
    own_copy.start()

    def w_copy(s, d):
        hops = n - 1 - s
        dest = at(pos + hops) if d == 0 else at(pos - hops)
        column = pl.multiple_of(dest * feats + d * half, half)
        return pltpu.make_async_copy(
            w.at[:, pl.ds(column, half)], wv.at[d, pl.ds(0, depth)], w_sem.at[d]
        )

    for d in range(2):
        w_copy(0, d).start()
    res_copy = pltpu.make_async_copy(res, rv, loc.at[1])
    res_copy.start()
    pl.semaphore_wait(barrier, n + 1)

    def x_copy(c):
        where = pl.ds(pl.multiple_of(c * part, part), part)
        return pltpu.make_async_remote_copy(
            src_ref=hid.at[where], dst_ref=xh.at[where],
            send_sem=x_send.at[c], recv_sem=x_recv.at[c],
            device_id=(across, t), device_id_type=MESH,
        )

    a_copy = pltpu.make_async_remote_copy(
        src_ref=a, dst_ref=asib, send_sem=sib_send.at[0], recv_sem=sib_recv.at[0],
        device_id=(sibling, t), device_id_type=MESH,
    )
    b_copy = pltpu.make_async_remote_copy(
        src_ref=b, dst_ref=bsib, send_sem=sib_send.at[1], recv_sem=sib_recv.at[1],
        device_id=(sibling, t), device_id_type=MESH,
    )
    x_copy(0).start()
    x_copy(1).start()
    a_copy.start()
    b_copy.start()
    acc[...] = jnp.zeros_like(acc)
    own_copy.wait()

    def partial(s, d):
        w_copy(s, d).wait()
        width = min(256, half)

        def columns(i, carry):
            where = pl.ds(pl.multiple_of(i * width, width), width)
            pv[d, :, where] = jnp.dot(
                hv[...], wv[d, pl.ds(0, depth), where], preferred_element_type=F32
            )
            return carry

        lax.fori_loop(0, half // width, columns, 0)

        @pl.when(s + 1 < n)
        def _():
            w_copy(s + 1, d).start()

    def adapter_of(i):
        theirs = i // tiles
        owner = g * (1 - theirs) + sibling * theirs
        return owner * residents + lax.rem(i, tiles) * per_tile

    def a_start(i, slot):
        @pl.when(i < tiles)
        def _():
            where = pl.ds(pl.multiple_of(lax.rem(i, tiles) * tile, tile), tile)
            pltpu.make_async_copy(a.at[where], av.at[slot], a_sem.at[slot]).start()

        @pl.when(i >= tiles)
        def _():
            where = pl.ds(pl.multiple_of(lax.rem(i, tiles) * tile, tile), tile)
            pltpu.make_async_copy(asib.at[where], av.at[slot], a_sem.at[slot]).start()

    def mix(first, count, rows_ref, column, width, ids_row):
        a_start(first, 0)

        def one(i, carry):
            @pl.when(i + 1 < count)
            def _():
                a_start(first + i + 1, lax.rem(i + 1, 2))

            slot = lax.rem(i, 2)
            pltpu.make_async_copy(
                a.at[pl.ds(0, tile)], av.at[slot], a_sem.at[slot]
            ).wait()
            products = lax.dot_general(
                av[slot], rows_ref[...], (((1,), (1,)), ((), ())),
                preferred_element_type=F32,
            )
            start = adapter_of(first + i)
            ids = idr[pl.ds(ids_row, 1), pl.ds(column, width)]
            where = pl.ds(pl.multiple_of(ids_row * rows + column, width), width)
            total = acc[:, where]
            for j in range(per_tile):
                total = total + jnp.where(
                    ids == start + j, products[j * rank:(j + 1) * rank], 0.0
                )
            acc[:, where] = total
            return carry

        lax.fori_loop(0, count, one, 0)

    def mix_across(c):
        x_copy(c).wait_recv()
        where = pl.ds(pl.multiple_of(c * part, part), part)
        copy = pltpu.make_async_copy(xh.at[where], xv, loc.at[2])
        copy.start()
        copy.wait()
        mix(0, 2 * tiles, xv, pl.multiple_of(c * part, part), part, 1)

    def ring_copy(s, d, h):
        where = pl.ds(h * sub, sub)
        return pltpu.make_async_remote_copy(
            src_ref=ring.at[d, s, where], dst_ref=ring.at[d, s + 1, where],
            send_sem=ring_send.at[d, s, h], recv_sem=ring_recv.at[d, s + 1, h],
            device_id=(g, toward[d]), device_id_type=MESH,
        )

    per_turn = 2 * tiles // X_PARTS

    def step(s, carry):
        for d in range(2):
            partial(s, d)

            @pl.when(s == 0)
            def _():
                for h in range(2):
                    where = pl.ds(h * sub, sub)
                    ring[d, 0, where] = pv[d, where].astype(BF16)
                    ring_copy(s, d, h).start()

        turn = s // 2

        @pl.when((lax.rem(s, 2) == 1) & (turn < X_PARTS))
        def _():
            mix(turn * per_turn, per_turn, hv, 0, rows, 0)

        @pl.when((lax.rem(s, 2) == 0) & (turn >= 1) & (turn < X_PARTS))
        def _():
            @pl.when(turn == 1)
            def _():
                a_copy.wait_recv()

            mix_across(turn - 1)

            @pl.when(turn + 1 < X_PARTS)
            def _():
                x_copy(turn + 1).start()

        @pl.when(s > 0)
        def _():
            for h in range(2):
                where = pl.ds(h * sub, sub)
                for d in range(2):
                    ring_copy(s - 1, d, h).wait_recv()

                    @pl.when(s < n - 1)
                    def _():
                        ring[d, s, where] = (
                            ring[d, s, where].astype(F32) + pv[d, where]
                        ).astype(BF16)
                        ring_copy(s, d, h).start()

                    @pl.when(s == n - 1)
                    def _():
                        pv[d, where] = ring[d, s, where].astype(F32) + pv[d, where]

        return carry

    lax.fori_loop(0, n, step, 0)

    b_copy.wait_recv()
    b_copies = []
    for d in range(2):
        for i, source in enumerate((b, bsib)):
            b_copies.append(
                pltpu.make_async_copy(
                    source.at[:, pl.ds(d * half, half)],
                    wv.at[d, pl.ds(i * a_rows, a_rows)],
                    loc.at[3 + 2 * d + i],
                )
            )
    for copy in b_copies:
        copy.start()
    mix_across(X_PARTS - 1)

    for q in range(n):
        mixb[q] = acc[:, q * block:(q + 1) * block].astype(BF16)

    def slice_out(q):
        return pltpu.make_async_remote_copy(
            src_ref=mixb.at[q], dst_ref=rs.at[t],
            send_sem=rs_send.at[q], recv_sem=rs_recv.at[t],
            device_id=(g, q), device_id_type=MESH,
        )

    def slice_in(q):
        return pltpu.make_async_copy(mixb.at[q], rs.at[q], rs_recv.at[q])

    def sum_out(q):
        return pltpu.make_async_remote_copy(
            src_ref=ag.at[t], dst_ref=ag.at[t],
            send_sem=ag_send.at[q], recv_sem=ag_recv.at[t],
            device_id=(g, q), device_id_type=MESH,
        )

    def sum_in(q):
        return pltpu.make_async_copy(mixb.at[q], ag.at[q], ag_recv.at[q])

    for k in range(1, n):
        slice_out(lax.rem(t + k, n)).start()
    total = mixb[t].astype(F32)
    for k in range(1, n):
        q = lax.rem(t + k, n)
        slice_in(q).wait()
        total = total + rs[q].astype(F32)
    ag[t] = total.astype(BF16)
    for k in range(1, n):
        sum_out(lax.rem(t + k, n)).start()
    for k in range(1, n):
        sum_in(lax.rem(t + k, n)).wait()
    for copy in b_copies:
        copy.wait()

    def delta(q, d_write):
        mixes = ag[q].astype(F32)
        wide = jnp.concatenate([mixes] * per_tile, axis=0).T.astype(BF16)
        ids = idc[pl.ds(pl.multiple_of(q * block, block), block), :]
        lane = lax.broadcasted_iota(jnp.int32, (block, tile), 1) // rank
        for i in range(2 * tiles):
            owner = g if i < tiles else sibling
            start = owner * residents + (i % tiles) * per_tile
            ev[:, i * tile:(i + 1) * tile] = jnp.where(
                ids == start + lane, wide, jnp.zeros_like(wide)
            )
        for d in range(2):
            d_write(
                d,
                jnp.dot(
                    ev[...], wv[d, pl.ds(0, 2 * a_rows)], preferred_element_type=F32
                ).astype(BF16),
            )

    def delta_copy(j):
        return pltpu.make_async_remote_copy(
            src_ref=dsend.at[j], dst_ref=drecv.at[j],
            send_sem=d_send.at[j], recv_sem=d_recv.at[j],
            device_id=(across, t), device_id_type=MESH,
        )

    def across_block(j, carry):
        def write(d, value):
            dsend[j, :, d * half:(d + 1) * half] = value

        delta(blocks + j, write)
        delta_copy(j).start()
        return carry

    lax.fori_loop(0, blocks, across_block, 0)
    res_copy.wait()

    def own_block(j, carry):
        where = pl.ds(pl.multiple_of(j * block, block), block)

        def write(d, value):
            pv[d, where] = pv[d, where] + value.astype(F32)

        delta(j, write)
        return carry

    lax.fori_loop(0, blocks, own_block, 0)

    def out_copy(j):
        where = pl.ds(pl.multiple_of(j * block, block), block)
        return pltpu.make_async_copy(rv.at[where], out.at[where], out_sem.at[j])

    def finish(j, carry):
        where = pl.ds(pl.multiple_of(j * block, block), block)
        delta_copy(j).wait_recv()
        for d in range(2):
            columns = slice(d * half, (d + 1) * half)
            rv[where, columns] = (
                rv[where, columns].astype(F32)
                + (pv[d, where] + drecv[j, :, columns].astype(F32))
            ).astype(BF16)
        out_copy(j).start()
        return carry

    lax.fori_loop(0, blocks, finish, 0)

    def drain(s, carry):
        for d in range(2):
            for h in range(2):
                ring_copy(s, d, h).wait_send()
        return carry

    lax.fori_loop(0, n - 1, drain, 0)
    for c in range(X_PARTS):
        x_copy(c).wait_send()
    a_copy.wait_send()
    b_copy.wait_send()
    for k in range(1, n):
        q = lax.rem(t + k, n)
        slice_out(q).wait_send()
        sum_out(q).wait_send()
    for j in range(blocks):
        delta_copy(j).wait_send()
        out_copy(j).wait()


def per_device(
    hidden, residual, down_projection_weight, adapter_down_maps, adapter_up_maps, row_adapter_index
):
    n, groups = lax.axis_size("tp"), lax.axis_size("group")
    rows, depth = hidden.shape
    feats = residual.shape[1]
    half = feats // 2
    residents, rank, _ = adapter_down_maps.shape
    a_rows = residents * rank
    tile = 4 * rank
    block, blocks = 2 * rows // n, n // 2
    ids = row_adapter_index[:, 0]
    swap = [(i, (i + groups // 2) % groups) for i in range(groups)]
    both = jnp.stack([ids, lax.ppermute(ids, "group", swap)])
    hbm = pl.BlockSpec(memory_space=pl.ANY)
    vmem = pl.BlockSpec(memory_space=pltpu.VMEM)
    dma = pltpu.SemaphoreType.DMA
    bf16 = functools.partial(jax.ShapeDtypeStruct, dtype=BF16)
    outs = pl.pallas_call(
        functools.partial(kernel, n, groups, rank, tile),
        out_shape=[
            bf16((rows, feats)), bf16((rows, depth)),
            bf16((a_rows, depth)), bf16((a_rows, feats)),
        ],
        in_specs=[vmem, vmem, hbm, hbm, hbm, hbm, hbm],
        out_specs=[hbm] * 4,
        scratch_shapes=[
            pltpu.VMEM((rows, depth), BF16),
            pltpu.VMEM((2, max(depth, 2 * a_rows), half), BF16),
            pltpu.VMEM((2, rows, half), F32),
            pltpu.VMEM((2, n, rows, half), BF16),
            pltpu.VMEM((2, tile, depth), BF16),
            pltpu.VMEM((rows // X_PARTS, depth), BF16),
            pltpu.VMEM((rank, 2 * rows), F32),
            pltpu.VMEM((block, 2 * a_rows), BF16),
            pltpu.VMEM((rows, feats), BF16),
            pltpu.VMEM((blocks, block, feats), BF16),
            pltpu.VMEM((blocks, block, feats), BF16),
            pltpu.VMEM((n, rank, block), BF16),
            pltpu.VMEM((n, rank, block), BF16),
            pltpu.VMEM((n, rank, block), BF16),
            dma((2, n, 2)), dma((2, n, 2)), dma((2,)), dma((2,)),
            dma((X_PARTS,)), dma((X_PARTS,)), dma((2,)), dma((2,)),
            dma((n,)), dma((n,)), dma((n,)), dma((n,)),
            dma((blocks,)), dma((blocks,)), dma((7,)), dma((blocks,)),
        ],
        compiler_params=pltpu.CompilerParams(
            collective_id=0, has_side_effects=True, vmem_limit_bytes=62 * 2**20
        ),
        cost_estimate=pl.CostEstimate(
            flops=2 * rows * depth * (n * feats + 4 * a_rows),
            bytes_accessed=2 * depth * n * feats,
            transcendentals=0,
        ),
        name="ring_and_adapters",
    )(
        both, both.reshape(2 * rows, 1), hidden, residual, down_projection_weight,
        adapter_down_maps.reshape(a_rows, depth), adapter_up_maps.reshape(a_rows, feats),
    )
    return outs[0]


def solution(mesh):
    in_specs = (
        P("group", "tp"),
        P("group", "tp"),
        P("tp", None),
        P("group", None, "tp"),
        P("group", None, "tp"),
        P("group", None),
    )
    return jax.shard_map(
        per_device, mesh=mesh, in_specs=in_specs, out_specs=P("group", "tp"), check_vma=False
    )
```

time: 501 us -> 281 us (0.56)
  waiting for transfers between devices: 291 us -> 1.79 us
  Pallas kernels: 0 us -> 270 us
  matrix products: 110 us -> 0 us
  blocking collectives: 43.1 us -> 0 us
  local copies, waits for them, and re-layouts: 37.2 us -> 4.44 us
  between operations: 14.9 us -> 0.01 us
    all_gather x2 -> x0, waiting for transfers between devices: 289 us -> none  [the longest x1 257 us: per_device(): lax.all_gather(adapter_down_maps, 'group', axis=0, tiled=True)]
    pallas_call x0 -> x1, Pallas kernels: none -> 270 us  [per_device(): pl.pallas_call(functools.partial(kernel, n, groups, rank, tile), out_shap...]
    dot_general x3 -> x0, matrix products: 110 us -> none  [the longest x1 68.9 us: per_device(): lax.dot_general(down_projection_weight, hidden, (((0,), (1,)), ((), ())),...]
    psum x1 -> x0, blocking collectives: 43.1 us -> none  [per_device(): lax.psum(partial_mix.reshape(adapter_total, MOST * rank_columns), 'tp')]
    scatter x1 -> x0, local copies, waits for them, and re-layouts: 19.7 us -> none  [per_device(): jnp.zeros((adapter_total * MOST, hidden_cols), jnp.bfloat16).at[slot_index]]
    gather x2 -> x0, local copies, waits for them, and re-layouts: 10.3 us -> none  [per_device(): delta_rows = delta_slots[slot_index]]
  transfers between devices with their start and end apart: 3 -> 1, of which waited for: 2 -> 1; matrix products, arithmetic and copies ran while one was open for 29% -> 0% of each run, Pallas kernels for 0% -> 0%
where the time goes in v1:
time: 281 us; the launch traced here: 280 us
  Pallas kernels  270 us (96%)
  local copies, waits for them, and re-layouts  4.44 us (2%)
  starting transfers between devices  2.94 us (1%)
    pallas_call x1, Pallas kernels, per_device(): pl.pallas_call(functools.partial(kernel, n, groups, rank, tile), out_shap...  270 us
  transfers between devices with their start and end apart: 1, of which 1 were waited for; matrix products, arithmetic and copies ran while one was open for 0% of the time, Pallas kernels for 0%

profile of v1, /device:TPU:0, one launch (start us, length us, event | category | flops | bytes accessed | tf_op | source)
XLA Modules:
  0.0 280.4 jit_solution(12281601491039685824)
XLA Ops:
  0.0 2.9 %collective-permute-start = (s32[1024]{0:T(1024)}, s32[1024]{0:T(1024)S(1)}, u32[]{:S(2)}, u32[]{:S(2)}) collective-permute-start(s32[1024]{0:T(1024)} %bitcast.12), channel_id=1, source_target_pairs={{0,16},{8,24},{16,0},{24,8},{1,17},{9,25},{17,1},{25,9},{2,18},{10... | collective-permute-start | bytes 12296 | tf_op jit(solution)/shard_map/ppermute | solution.py:380
  2.9 1.8 collective-permute-done
  4.7 1.3 fusion
  6.0 1.3 copy.9
  7.4 270.0 %ring_and_adapters.1 = (bf16[1024,1024]{1,0:T(8,128)(2,1)}, bf16[1024,3584]{1,0:T(8,128)(2,1)}, bf16[2048,3584]{1,0:T(8,128)(2,1)}, bf16[2048,1024]{1,0:T(8,128)(2,1)}) custom-call(s32[2,1024]{1,0:T(2,128)} %get-tuple-element.8.idr, s32[2048,1]{1,0:T(8,128)} %bitcast.10, bf16[1024,3584]{1,0:T(8,128)(2,1)} %hid.1, bf16[1024,1024]{1,0:T(8,128)(2,1)} %res.1, ...), custom_call_target="tpu_custom_call" | custom-call | flops 120259084288 | bytes 58720256 | tf_op jit(solution)/shard_map/ring_and_adapters/pallas_call | solution.py:385
  277.4 3.1 %copy.11 = bf16[1024,1024]{1,0:T(8,128)(2,1)} copy(bf16[1024,1024]{1,0:T(8,128)(2,1)} %get-tuple-element.6) | data formatting | bytes 4194304
  (1 shorter events, 0.0 us)
Async XLA Ops:
  0.0 4.7 %collective-permute-start = (s32[1024]{0:T(1024)}, s32[1024]{0:T(1024)S(1)}, u32[]{:S(2)}, u32[]{:S(2)}) collective-permute-start(s32[1024]{0:T(1024)} %bitcast.12), channel_id=1, source_target_pairs={{0,16},{8,24},{16,0},{24,8},{1,17},{9,25},{17,1},{25,9},{2,18},{10... | collective-permute-start | bytes 12296 | tf_op jit(solution)/shard_map/ppermute | solution.py:380

commit v2 on v1

--- a/solution.py
+++ b/solution.py
@@ -238,10 +238,6 @@
             )
     for copy in b_copies:
         copy.start()
-    mix_across(X_PARTS - 1)
-
-    for q in range(n):
-        mixb[q] = acc[:, q * block:(q + 1) * block].astype(BF16)
 
     def slice_out(q):
         return pltpu.make_async_remote_copy(
@@ -263,8 +259,18 @@
     def sum_in(q):
         return pltpu.make_async_copy(mixb.at[q], ag.at[q], ag_recv.at[q])
 
-    for k in range(1, n):
-        slice_out(lax.rem(t + k, n)).start()
+    def send_slices(first, last):
+        for q in range(first, last):
+            mixb[q] = acc[:, q * block:(q + 1) * block].astype(BF16)
+
+            @pl.when(t != q)
+            def _():
+                slice_out(q).start()
+
+    early = (2 * rows - part) // block
+    send_slices(0, early)
+    mix_across(X_PARTS - 1)
+    send_slices(early, n)
     total = mixb[t].astype(F32)
     for k in range(1, n):
         q = lax.rem(t + k, n)
@@ -373,7 +379,7 @@
     half = feats // 2
     residents, rank, _ = adapter_down_maps.shape
     a_rows = residents * rank
-    tile = 4 * rank
+    tile = 8 * rank
     block, blocks = 2 * rows // n, n // 2
     ids = row_adapter_index[:, 0]
     swap = [(i, (i + groups // 2) % groups) for i in range(groups)]

time: 281 us -> 261 us (0.929)
  Pallas kernels: 270 us -> 250 us
    pallas_call x1, Pallas kernels: 270 us -> 250 us  [per_device(): pl.pallas_call(functools.partial(kernel, n, groups, rank, tile), out_shap...]
where the time goes in v2:
time: 261 us
  Pallas kernels  250 us (96%)
  local copies, waits for them, and re-layouts  4.44 us (2%)
  starting transfers between devices  2.94 us (1%)
    pallas_call x1, Pallas kernels, per_device(): pl.pallas_call(functools.partial(kernel, n, groups, rank, tile), out_shap...  250 us
  transfers between devices with their start and end apart: 1, of which 1 were waited for; matrix products, arithmetic and copies ran while one was open for 0% of the time, Pallas kernels for 0%

profile of v2, /device:TPU:0, one launch (start us, length us, event | category | flops | bytes accessed | tf_op | source)
XLA Modules:
  0.0 260.5 jit_solution(13154366985643842988)
XLA Ops:
  0.0 2.9 %collective-permute-start = (s32[1024]{0:T(1024)}, s32[1024]{0:T(1024)S(1)}, u32[]{:S(2)}, u32[]{:S(2)}) collective-permute-start(s32[1024]{0:T(1024)} %bitcast.12), channel_id=1, source_target_pairs={{0,16},{8,24},{16,0},{24,8},{1,17},{9,25},{17,1},{25,9},{2,18},{10... | collective-permute-start | bytes 12296 | tf_op jit(solution)/shard_map/ppermute | solution.py:386
  2.9 1.8 collective-permute-done
  4.7 1.3 fusion
  6.0 1.3 copy.9
  7.4 250.1 %ring_and_adapters.1 = (bf16[1024,1024]{1,0:T(8,128)(2,1)}, bf16[1024,3584]{1,0:T(8,128)(2,1)}, bf16[2048,3584]{1,0:T(8,128)(2,1)}, bf16[2048,1024]{1,0:T(8,128)(2,1)}) custom-call(s32[2,1024]{1,0:T(2,128)} %get-tuple-element.8.idr, s32[2048,1]{1,0:T(8,128)} %bitcast.10, bf16[1024,3584]{1,0:T(8,128)(2,1)} %hid.1, bf16[1024,1024]{1,0:T(8,128)(2,1)} %res.1, ...), custom_call_target="tpu_custom_call" | custom-call | flops 120259084288 | bytes 58720256 | tf_op jit(solution)/shard_map/ring_and_adapters/pallas_call | solution.py:391
  257.4 3.1 %copy.11 = bf16[1024,1024]{1,0:T(8,128)(2,1)} copy(bf16[1024,1024]{1,0:T(8,128)(2,1)} %get-tuple-element.6) | data formatting | bytes 4194304
  (1 shorter events, 0.0 us)
Async XLA Ops:
  0.0 4.7 %collective-permute-start = (s32[1024]{0:T(1024)}, s32[1024]{0:T(1024)S(1)}, u32[]{:S(2)}, u32[]{:S(2)}) collective-permute-start(s32[1024]{0:T(1024)} %bitcast.12), channel_id=1, source_target_pairs={{0,16},{8,24},{16,0},{24,8},{1,17},{9,25},{17,1},{25,9},{2,18},{10... | collective-permute-start | bytes 12296 | tf_op jit(solution)/shard_map/ppermute | solution.py:386
